TPU v7x, 256 devices: a whole 4x4x8 slice. The times are simulated.
256 devices in a mesh: frame: 32 (over x, z), head: 8 (over y, core).
Axes of the slice: x: 4, y: 4, z: 8, core: 2. Of those that a mesh axis runs over, the one named last changes fastest.
Arguments:
- queries: bfloat16 [32, 1024, 3072], P('frame', None, 'head'), may hold values from -8 to 8
- keys: bfloat16 [32, 1024, 3072], P('frame', None, 'head'), may hold values from -8 to 8
- values: bfloat16 [32, 1024, 3072], P('frame', None, 'head'), may hold values from -6 to 6
- out_weight: bfloat16 [3072, 3072], P('head'), may hold values from -0.15625 to 0.15625
- head_class: int32 [24], P('head'), may hold values from 0 to 1, as said below
- sink_frame: int32 [24], P('head'), may hold values from 0 to 31
Outputs:
- mixed: bfloat16 [32, 1024, 3072], P('frame', None, 'head')
Inputs may be any that keep to these rules, and one draw needn't show every extreme that they name: `head_class`: in each block of 3 consecutive heads, 1 to 2 heads are temporal (1) and the rest spatial (0), so at most 2 are spatial; blocks with 1 and blocks with 2 temporal heads both occur.
All inputs are finite; a program needn't handle non-finite values.
Results may differ from a plain program's by a relative error of at most 0.017.
Values may be sent and summed in bfloat16 or wider, within the bound.
A program may use at most 64 MiB of HBM per device.

v0:
```python
import math

import jax
import jax.numpy as jnp
from jax import lax
from jax.sharding import PartitionSpec as P


def broadcast(value, axis, source):
    kept = jnp.where(lax.axis_index(axis) == source, value, 0).astype(value.dtype)
    return lax.psum(kept, axis)


def pick_heads(data, slots, head_dim):
    return jnp.stack(
        [
            lax.dynamic_slice_in_dim(data, slots[j] * head_dim, head_dim, 1)
            for j in range(slots.shape[0])
        ],
        1,
    )


def attend(query, keys, values, scale):
    scores = jnp.dot(query, keys.T, preferred_element_type=jnp.float32) * scale
    top = jnp.max(scores, axis=-1, keepdims=True)
    weights = jnp.exp(scores - top)
    total = jnp.sum(weights, axis=-1, keepdims=True)
    mixed = (
        jnp.dot(weights.astype(jnp.bfloat16), values, preferred_element_type=jnp.float32) / total
    )
    return mixed.astype(jnp.bfloat16)


def temporal_heads(items, scale):
    query, keys, values = items
    scores = jnp.einsum("fphd,gphd->phfg", query, keys, preferred_element_type=jnp.float32) * scale
    top = jnp.max(scores, axis=-1, keepdims=True)
    weights = jnp.exp(scores - top)
    total = jnp.sum(weights, axis=-1)
    mixed = jnp.einsum(
        "phfg,gphd->fphd", weights.astype(jnp.bfloat16), values, preferred_element_type=jnp.float32
    )
    return (mixed / jnp.transpose(total, (2, 0, 1))[..., None]).astype(jnp.bfloat16)


def per_device(queries, keys, values, out_weight, head_class, sink_frame):
    heads_here = head_class.shape[0]
    head_dim = queries.shape[2] // heads_here
    scale = head_dim ** (-0.5)
    local_q = queries[0]
    local_k = keys[0]
    local_v = values[0]
    tokens = local_q.shape[0]
    order = jnp.arange(heads_here, dtype=jnp.int32)
    spat_q = pick_heads(local_q, order, head_dim)
    spat_k = pick_heads(local_k, order, head_dim)
    spat_v = pick_heads(local_v, order, head_dim)
    block = math.gcd(tokens, 512)
    results = []
    for slot in range(order.shape[0]):
        root = sink_frame[order[slot]]
        sink_k, sink_v = (
            broadcast(spat_k[:, slot], "frame", root),
            broadcast(spat_v[:, slot], "frame", root),
        )
        keys_one = jnp.concatenate([spat_k[:, slot], sink_k], axis=0)
        values_one = jnp.concatenate([spat_v[:, slot], sink_v], axis=0)

        def one_block(rows, keys_one=keys_one, values_one=values_one):
            return attend(rows, keys_one, values_one, scale)

        rows_all = spat_q[:, slot].reshape(tokens // block, block, head_dim)
        results.append(lax.map(one_block, rows_all).reshape(tokens, head_dim))
    spatial = jnp.stack(results, 1)
    mixed_here = temporal_heads(
        (
            lax.all_to_all(
                pick_heads(local_q, order, head_dim)[None],
                "frame",
                split_axis=1,
                concat_axis=0,
                tiled=True,
            ),
            lax.all_to_all(
                pick_heads(local_k, order, head_dim)[None],
                "frame",
                split_axis=1,
                concat_axis=0,
                tiled=True,
            ),
            lax.all_to_all(
                pick_heads(local_v, order, head_dim)[None],
                "frame",
                split_axis=1,
                concat_axis=0,
                tiled=True,
            ),
        ),
        scale,
    )
    temporal = lax.all_to_all(mixed_here, "frame", split_axis=0, concat_axis=1, tiled=True)[0]
    is_temp = head_class == 1
    spat_select = (
        (order[:, None] == order[None, :]) & jnp.logical_not(is_temp[order])[:, None]
    ).astype(jnp.bfloat16)
    temp_select = ((order[:, None] == order[None, :]) & is_temp[order][:, None]).astype(
        jnp.bfloat16
    )
    combined = jnp.einsum("pjd,jh->phd", spatial, spat_select, preferred_element_type=jnp.float32)
    combined = combined + jnp.einsum(
        "pjd,jh->phd", temporal, temp_select, preferred_element_type=jnp.float32
    )
    combined = combined.astype(jnp.bfloat16).reshape(tokens, heads_here * head_dim)
    partial_value = jnp.dot(combined, out_weight, preferred_element_type=jnp.float32)
    summed = lax.psum_scatter(
        partial_value.astype(jnp.bfloat16), "head", scatter_dimension=1, tiled=True
    )
    return summed[None]


def solution(mesh):
    placed = (
        P("frame", None, "head"),
        P("frame", None, "head"),
        P("frame", None, "head"),
        P("head", None),
        P("head"),
        P("head"),
    )
    return jax.shard_map(
        per_device, mesh=mesh, in_specs=placed, out_specs=P("frame", None, "head"), check_vma=False
    )
```

profile of v0, /device:TPU:1, one launch (start us, length us, event | category | flops | bytes accessed | tf_op | source)
XLA Modules:
  0.0 379.8 jit_solution(11385850303601492922)
XLA Ops:
  12.8 12.0 %all-to-all-start.1 = ((bf16[1,1024,3,128]{3,2,0,1:T(4,128)(2,1)}), bf16[1,1024,3,128]{3,2,0,1:T(4,128)(2,1)}, u32[]{:S(2)}, u32[]{:S(2)}) async-start(bf16[1,1024,3,128]{3,2,0,1:T(4,128)(2,1)} %copy.54), calls=%async_computation.1 | async-start | bytes 2097152 | tf_op jit(solution)/shard_map/all_to_all | solution.py:78
  24.8 2.2 dynamic-slice_bitcast_fusion.8
  28.8 20.7 %all-to-all-done.1 = bf16[1,1024,3,128]{3,2,0,1:T(4,128)(2,1)} async-done(((bf16[1,1024,3,128]{3,2,0,1:T(4,128)(2,1)}), bf16[1,1024,3,128]{3,2,0,1:T(4,128)(2,1)}, u32[]{:S(2)}, u32[]{:S(2)}) %all-to-all-start.1) | async-done | bytes 786464 | tf_op jit(solution)/shard_map/all_to_all | solution.py:78
  49.4 8.7 %all-to-all-start.2 = ((bf16[1,1024,3,128]{3,2,0,1:T(4,128)(2,1)}), bf16[1,1024,3,128]{3,2,0,1:T(4,128)(2,1)}, u32[]{:S(2)}, u32[]{:S(2)}) async-start(bf16[1,1024,3,128]{3,2,0,1:T(4,128)(2,1)} %copy.56), calls=%async_computation.2 | async-start | bytes 2097152 | tf_op jit(solution)/shard_map/all_to_all | solution.py:85
  60.9 22.0 %all-to-all-done.2 = bf16[1,1024,3,128]{3,2,0,1:T(4,128)(2,1)} async-done(((bf16[1,1024,3,128]{3,2,0,1:T(4,128)(2,1)}), bf16[1,1024,3,128]{3,2,0,1:T(4,128)(2,1)}, u32[]{:S(2)}, u32[]{:S(2)}) %all-to-all-start.2) | async-done | bytes 786464 | tf_op jit(solution)/shard_map/all_to_all | solution.py:85
  82.9 8.6 %all-to-all-start = ((bf16[1,1024,3,128]{3,2,0,1:T(4,128)(2,1)}), bf16[1,1024,3,128]{3,2,0,1:T(4,128)(2,1)}, u32[]{:S(2)}, u32[]{:S(2)}) async-start(bf16[1,1024,3,128]{3,2,0,1:T(4,128)(2,1)} %copy.52), calls=%async_computation | async-start | bytes 2097152 | tf_op jit(solution)/shard_map/all_to_all | solution.py:92
  99.7 3.2 broadcast_select_fusion.4
  103.6 3.1 fusion.96
  108.4 7.9 %all-to-all-done = bf16[1,1024,3,128]{3,2,0,1:T(4,128)(2,1)} async-done(((bf16[1,1024,3,128]{3,2,0,1:T(4,128)(2,1)}), bf16[1,1024,3,128]{3,2,0,1:T(4,128)(2,1)}, u32[]{:S(2)}, u32[]{:S(2)}) %all-to-all-start) | async-done | bytes 786464 | tf_op jit(solution)/shard_map/all_to_all | solution.py:92
  116.2 3.0 fusion.69
  120.4 8.6 %all-to-all-start.3 = ((bf16[32,32,3,128]{3,1,2,0:T(8,128)(2,1)}), bf16[32,32,3,128]{3,1,2,0:T(8,128)(2,1)}, u32[]{:S(2)}, u32[]{:S(2)}) async-start(bf16[32,32,3,128]{3,1,2,0:T(8,128)(2,1)} %copy.62), calls=%async_computation.3 | async-start | bytes 1572864 | tf_op jit(solution)/shard_map/all_to_all | solution.py:102
  129.3 133.7 %all-reduce.3.cloned.1.call-done = (bf16[1024,128]{1,0:T(8,128)(2,1)}, bf16[1024,128]{1,0:T(8,128)(2,1)}, bf16[1024,128]{1,0:T(8,128)(2,1)}, bf16[1024,128]{1,0:...) async-done(((bf16[1024,128]{1,0:T(8,128)(2,1)}, bf16[1024,128]{1,0:T(8,128)(2,1)}, bf16[1024,128]{1,0:T(8,128)(2,1)}, bf16[1024,128]{1,0:T(8,128)(2,1)}, ...) | async-done | bytes 1572880 | tf_op jit(solution)/shard_map/psum | solution.py:11
  266.6 8.4 %while.32 = (s32[]{:T(128)}, bf16[2,512,128]{2,1,0:T(8,128)(2,1)}, bf16[2,512,128]{2,1,0:T(8,128)(2,1)}, bf16[2048,128]{1,0:T(8,128)(2,1)S(1)}, bf16[2048,128]{1,0:T(8,128)(2,1)}, /*index=5*/s32[]{:T(128)}) while((s32[]{:T(128)}, bf16[2,512,128]{2,1,0:T(8,128)(2,1)}, bf16[2,512,128]{2,1,0:T(8,128)(2,1)}, bf16[2048,128]{1,0:T(8,128)(2,1)S(1)}, ...), condition=%wide.region_17.18_spmd, body=%wide.region_14.17_spmd.sunk | while | flops 545389568 | bytes 18098344 | solution.py:74
  275.1 2.1 copy.51
  280.9 6.5 %while.31 = (s32[]{:T(128)}, bf16[2,512,128]{2,1,0:T(8,128)(2,1)}, bf16[2,512,128]{2,1,0:T(8,128)(2,1)S(1)}, bf16[2048,128]{1,0:T(8,128)(2,1)S(1)}, bf16[2048,128]{1,0:T(8,128)(2,1)}, /*index=5*/s32[]{:T(128)}) while((s32[]{:T(128)}, bf16[2,512,128]{2,1,0:T(8,128)(2,1)}, bf16[2,512,128]{2,1,0:T(8,128)(2,1)S(1)}, ...), condition=%wide.region_11.12_spmd, body=%wide.region_8.11_spmd.sunk | while | flops 545389568 | bytes 18098344 | solution.py:74
  287.3 2.2 copy.50
  292.5 5.1 %while.30 = (s32[]{:T(128)}, bf16[2,512,128]{2,1,0:T(8,128)(2,1)S(1)}, bf16[2,512,128]{2,1,0:T(8,128)(2,1)S(1)}, bf16[2048,128]{1,0:T(8,128)(2,1)S(1)}, bf16[2048,128]{1,0:T(8,128)(2,1)}, /*index=5*/s32[]{:T(128)}) while((s32[]{:T(128)}, bf16[2,512,128]{2,1,0:T(8,128)(2,1)S(1)}, bf16[2,512,128]{2,1,0:T(8,128)(2,1)S(1)}, ...), condition=%wide.region_5.6_spmd, body=%wide.region_2.5_spmd.sunk | while | flops 545389568 | bytes 16001137 | solution.py:74
  298.0 4.4 %fusion.73 = f32[3,1024,128]{2,0,1:T(4,128)} fusion(bf16[1024,1,128]{2,1,0:T(2,128)(2,1)} %copy.51, bf16[1024,1,128]{2,1,0:T(2,128)(2,1)} %copy.50, bf16[1024,1,128]{2,1,0:T(2,128)(2,1)S(1)} %copy.49, pred[3]{0:T(512)(128)(4,1)S(1)} %not.7), kind=kOutput, calls=%fused_computation.58 | convolution fusion | flops 4718610 | bytes 2359299 | tf_op jit(solution)/shard_map/pjd,jh->phd/dot_general | solution.py:110
  303.6 3.5 fusion.72
  307.1 2.3 copy.65
  309.3 6.5 %convolution_convert_fusion = bf16[1024,3072]{1,0:T(8,128)(2,1)} fusion(bf16[1024,384]{0,1:T(8,128)(2,1)} %bitcast.142, bf16[384,3072]{1,0:T(8,128)(2,1)S(1)} %copy-done), kind=kOutput, calls=%fused_computation.49 | convolution fusion | flops 2419064832 | bytes 9437184 | tf_op jit(solution)/shard_map/dot_general | solution.py:115
  315.9 8.6 %copy.73 = bf16[1024,3072]{0,1:T(8,128)(2,1)} copy(bf16[1024,3072]{1,0:T(8,128)(2,1)} %convolution_convert_fusion) | data formatting | bytes 12582912
  324.5 46.2 %reduce-scatter.4.cloned.1.call-done = bf16[384,1024]{1,0:T(8,128)(2,1)} async-done(((bf16[3072,1024]{1,0:T(8,128)(2,1)}), bf16[384,1024]{1,0:T(8,128)(2,1)}) %reduce-scatter.4.cloned.1.call-update) | async-done | bytes 786448
  370.7 2.3 copy.74
  (89 shorter events, 44.9 us)
Async XLA Ops:
  6.5 302.8 %copy-start = (bf16[384,3072]{1,0:T(8,128)(2,1)S(1)}, bf16[384,3072]{1,0:T(8,128)(2,1)}, u32[]{:S(2)}) copy-start(bf16[384,3072]{1,0:T(8,128)(2,1)} %param.15) | copy-start | bytes 7077892
  10.3 0.7 copy-start.2
  12.8 36.6 %all-to-all-start.1 = ((bf16[1,1024,3,128]{3,2,0,1:T(4,128)(2,1)}), bf16[1,1024,3,128]{3,2,0,1:T(4,128)(2,1)}, u32[]{:S(2)}, u32[]{:S(2)}) async-start(bf16[1,1024,3,128]{3,2,0,1:T(4,128)(2,1)} %copy.54), calls=%async_computation.1 | async-start | bytes 2097152 | tf_op jit(solution)/shard_map/all_to_all | solution.py:78
  28.8 68.5 %copy-start.10 = (s32[3]{0:T(128)S(1)}, s32[3]{0:T(128)}, u32[]{:S(2)}) copy-start(s32[3]{0:T(128)} %param.17) | copy-start | bytes 40
  49.4 33.5 %all-to-all-start.2 = ((bf16[1,1024,3,128]{3,2,0,1:T(4,128)(2,1)}), bf16[1,1024,3,128]{3,2,0,1:T(4,128)(2,1)}, u32[]{:S(2)}, u32[]{:S(2)}) async-start(bf16[1,1024,3,128]{3,2,0,1:T(4,128)(2,1)} %copy.56), calls=%async_computation.2 | async-start | bytes 2097152 | tf_op jit(solution)/shard_map/all_to_all | solution.py:85
  60.9 42.1 %copy-start.11 = (s32[3]{0:T(128)S(1)}, s32[3]{0:T(128)}, u32[]{:S(2)}) copy-start(s32[3]{0:T(128)} %param.16) | copy-start | bytes 40
  82.9 33.3 %all-to-all-start = ((bf16[1,1024,3,128]{3,2,0,1:T(4,128)(2,1)}), bf16[1,1024,3,128]{3,2,0,1:T(4,128)(2,1)}, u32[]{:S(2)}, u32[]{:S(2)}) async-start(bf16[1,1024,3,128]{3,2,0,1:T(4,128)(2,1)} %copy.52), calls=%async_computation | async-start | bytes 2097152 | tf_op jit(solution)/shard_map/all_to_all | solution.py:92
  91.5 171.5 %all-reduce.3.cloned.1.call-start = ((), (), s32[]{:S(2)}) async-start(), calls=%async_computation.6 | async-start | bytes 3145728 | tf_op jit(solution)/shard_map/psum | solution.py:11
  106.7 1.2 copy-start.1
  120.4 182.0 %all-to-all-start.3 = ((bf16[32,32,3,128]{3,1,2,0:T(8,128)(2,1)}), bf16[32,32,3,128]{3,1,2,0:T(8,128)(2,1)}, u32[]{:S(2)}, u32[]{:S(2)}) async-start(bf16[32,32,3,128]{3,1,2,0:T(8,128)(2,1)} %copy.62), calls=%async_computation.3 | async-start | bytes 1572864 | tf_op jit(solution)/shard_map/all_to_all | solution.py:102
  129.1 241.7 %reduce-scatter.4.cloned.1.call-start = ((), (), s32[]{:S(2)}) async-start(), calls=%async_computation.5 | async-start | bytes 7077888
  266.6 2.6 copy-start.3
  266.6 2.6 copy-start.8
  270.1 0.7 copy-start.4
  270.9 2.6 copy-start.3
  270.9 2.6 copy-start.8
  274.4 0.7 copy-start.4
  280.9 1.6 copy-start.5
  280.9 1.6 copy-start.9
  283.4 0.7 copy-start.6
  284.1 1.6 copy-start.5
  284.1 1.6 copy-start.9
  292.5 1.6 copy-start.7
  295.0 1.6 copy-start.7
  (1 other events, 0.7 us)
Sparse Core Ops, SparseCore 0:
  103.1 159.8 all-reduce.2
  324.6 46.0 reduce-scatter.3
where the time goes:
time: 381 us; the launch traced here: 380 us
  waiting for transfers between devices  230 us (60%)
  starting transfers between devices  38.2 us (10%)
  local copies, waits for them, and re-layouts  36.7 us (10%)
  matrix products  32.5 us (9%)
  between operations  23.1 us (6%)
  other arithmetic  18.6 us (5%)
    psum x1, waiting for transfers between devices, broadcast(): return lax.psum(kept, axis)  134 us
    unnamed x3, waiting for transfers between devices  46.2 us
    all_to_all x1, waiting for transfers between devices, per_device(): lax.all_to_all(pick_heads(local_k, order, head_dim)[None], 'frame', split...  22 us
    all_to_all x1, waiting for transfers between devices, per_device(): lax.all_to_all(pick_heads(local_q, order, head_dim)[None], 'frame', split...  20.7 us
    unnamed x12, local copies, waits for them, and re-layouts  12.8 us
    all_to_all x1, starting transfers between devices, per_device(): lax.all_to_all(pick_heads(local_q, order, head_dim)[None], 'frame', split...  12 us
    all_to_all x1, starting transfers between devices, per_device(): lax.all_to_all(pick_heads(local_k, order, head_dim)[None], 'frame', split...  8.71 us
    all_to_all x1, starting transfers between devices, per_device(): lax.all_to_all(mixed_here, 'frame', split_axis=0, concat_axis=1, tiled=True)  8.64 us
  transfers between devices with their start and end apart: 6, of which 5 were waited for; matrix products, arithmetic and copies ran while one was open for 15% of the time, Pallas kernels for 0%

commit v1 on v0

v1 whole, which is shorter than its diff:
```python
import math

import jax
import jax.numpy as jnp
from jax import lax
from jax.experimental import pallas as pl
from jax.experimental.pallas import tpu as pltpu
from jax.sharding import PartitionSpec as P

MESH = pl.DeviceIdType.MESH
NX, NZ, NY, NC = 4, 8, 4, 2
NF, NH = NX * NZ, NY * NC
TOK, HD, WID = 1024, 128, 384
HALF = TOK // 2
POS = HALF // NF
SLOT_A, SLOT_C, SLOT_B = 0, 1, 2
SCALE = HD ** (-0.5) * math.log2(math.e)


def first_with(cls, kind):
    return jnp.where(cls[0] == kind, 0, jnp.where(cls[1] == kind, 1, 2))


def softmax_times(scores, values):
    top = jnp.max(scores, axis=-1, keepdims=True)
    weights = jnp.exp2((scores - top) * SCALE)
    total = jnp.sum(weights, axis=-1, keepdims=True)
    mixed = jnp.dot(weights.astype(jnp.bfloat16), values, preferred_element_type=jnp.float32)
    return (mixed / total).astype(jnp.bfloat16)


def dot_nt(a, b):
    return lax.dot_general(a, b, (((1,), (1,)), ((), ())), preferred_element_type=jnp.float32)


def kernel(
    cls,
    sink,
    q_hbm,
    k_hbm,
    v_hbm,
    w_hbm,
    out_ref,
    vq,
    vk,
    vv,
    vw,
    xs,
    xr,
    os,
    tc,
    g,
    ws,
    wg,
    acc,
    ss,
    rx,
    qz,
    rz,
    sk,
    kv,
    sc,
    in_sem,
    fs_sem,
    fr_sem,
    bs_sem,
    br_sem,
    ws_sem,
    wr_sem,
    ks_sem,
    kr_sem,
    ys_sem,
    yr_sem,
    cs_sem,
    cr_sem,
):
    f = lax.axis_index("frame")
    h = lax.axis_index("head")
    mx, mz, my, mc = f // NZ, f % NZ, h // NC, h % NC

    ins = []
    for n, (src, dst) in enumerate(((k_hbm, vk), (v_hbm, vv), (q_hbm, vq))):
        for j in range(3):
            cp = pltpu.make_async_copy(
                src.at[0, :, pl.ds(j * HD, HD)], dst.at[j], in_sem.at[n * 3 + j]
            )
            cp.start()
            ins.append(cp)
    for j in range(3):
        cp = pltpu.make_async_copy(w_hbm.at[pl.ds(j * HD, HD)], vw.at[j], in_sem.at[9 + j])
        cp.start()
        ins.append(cp)

    barrier = pltpu.get_barrier_semaphore()

    def greet_frame(d, carry):
        pl.semaphore_signal(
            barrier, inc=1, device_id=(lax.rem(f + d, NF), h), device_id_type=MESH
        )
        return carry

    def greet_head(d, carry):
        pl.semaphore_signal(
            barrier, inc=1, device_id=(f, lax.rem(h + d, NH)), device_id_type=MESH
        )
        return carry

    lax.fori_loop(1, NF, greet_frame, 0)
    lax.fori_loop(1, NH, greet_head, 0)

    ia = first_with(cls, 1)
    ib = first_with(cls, 0)
    ic = 3 - ia - ib
    c_temp = cls[ic] == 1
    head_of = {SLOT_A: ia, SLOT_B: ib, SLOT_C: ic}
    spat = (SLOT_B, SLOT_C)

    for n in range(6):
        ins[n].wait()
    for s, slot in enumerate(spat):
        ss[:, s, 0] = vk[head_of[slot]].reshape(NX, TOK // NX, HD)
        ss[:, s, 1] = vv[head_of[slot]].reshape(NX, TOK // NX, HD)
        kv[s, 0, pl.ds(0, TOK)] = vk[head_of[slot]]
        kv[s, 1, pl.ds(0, TOK)] = vv[head_of[slot]]
    for n in range(6, 9):
        ins[n].wait()
    for slot in (SLOT_A, SLOT_C):
        for half in range(2):
            u = slot * 2 + half
            for t, src in enumerate((vq, vk, vv)):
                part = src[head_of[slot], pl.ds(half * HALF, HALF)]
                xs[u, :, t] = part.reshape(NF, POS, HD)
            xr[u, f] = xs[u, f]
    for n in range(9, 12):
        ins[n].wait()
    for slot in (SLOT_A, SLOT_C, SLOT_B):
        for p in range(NH):
            ws[p, slot] = vw[head_of[slot], :, pl.ds(p * WID, WID)]
    for slot in (SLOT_A, SLOT_C, SLOT_B):
        wg[slot, h] = ws[h, slot]
    for s in range(2):
        rx[mx, s] = ss[mx, s]

    pl.semaphore_wait(barrier, NF - 1 + NH - 1)

    def send_unit(u):
        def one(d, carry):
            p = lax.rem(f + d, NF)
            pltpu.make_async_remote_copy(
                src_ref=xs.at[u, p],
                dst_ref=xr.at[u, f],
                send_sem=fs_sem.at[u],
                recv_sem=fr_sem.at[u],
                device_id=(p, h),
                device_id_type=MESH,
            ).start()
            return carry

        lax.fori_loop(1, NF, one, 0)

    def return_unit(u):
        def one(d, carry):
            p = lax.rem(f + d, NF)
            dst = g.at[SLOT_A, h, u, f] if u < 2 else tc.at[u - 2, f]
            pltpu.make_async_remote_copy(
                src_ref=os.at[u, p],
                dst_ref=dst,
                send_sem=bs_sem.at[u],
                recv_sem=br_sem.at[u],
                device_id=(p, h),
                device_id_type=MESH,
            ).start()
            return carry

        lax.fori_loop(1, NF, one, 0)

    def wait_bytes(ref, sem):
        pltpu.make_async_copy(ref, ref, sem).wait()

    def x_peer(d):
        return lax.rem(mx + d, NX)

    def z_peer(d):
        return lax.rem(mz + d, NZ)

    for d in (1, 3, 2):
        pltpu.make_async_remote_copy(
            src_ref=ss.at[x_peer(d)],
            dst_ref=rx.at[mx],
            send_sem=ks_sem.at[0],
            recv_sem=kr_sem.at[0],
            device_id=(x_peer(d) * NZ + mz, h),
            device_id_type=MESH,
        ).start()
    send_unit(0)

    def send_weights(d, carry):
        p = lax.rem(h + d, NH)
        pltpu.make_async_remote_copy(
            src_ref=ws.at[p],
            dst_ref=wg.at[:, h],
            send_sem=ws_sem,
            recv_sem=wr_sem,
            device_id=(f, p),
            device_id_type=MESH,
        ).start()
        return carry

    lax.fori_loop(1, NH, send_weights, 0)

    root = [sink[head_of[slot]] for slot in spat]
    wait_bytes(rx.at[pl.ds(0, NX - 1)], kr_sem.at[0])
    for s in range(2):
        for t in range(2):
            qz[:, s, t] = rx[root[s] // NZ, s, t].reshape(NZ, TOK // NF, HD)
    rz[mz] = qz[mz]
    for d in (1, 7, 2, 6, 3, 5, 4):
        pltpu.make_async_remote_copy(
            src_ref=qz.at[z_peer(d)],
            dst_ref=rz.at[mz],
            send_sem=ks_sem.at[1],
            recv_sem=kr_sem.at[1],
            device_id=(mx * NZ + z_peer(d), h),
            device_id_type=MESH,
        ).start()
    send_unit(1)
    wait_bytes(rz.at[pl.ds(0, NZ - 1)], kr_sem.at[1])
    for s in range(2):
        sk[mx, mz, s] = rz[root[s] % NZ, s]
    for d in (1, 7, 2, 6, 3, 5, 4):
        pltpu.make_async_remote_copy(
            src_ref=sk.at[mx, mz],
            dst_ref=sk.at[mx, mz],
            send_sem=ks_sem.at[2],
            recv_sem=kr_sem.at[2],
            device_id=(mx * NZ + z_peer(d), h),
            device_id_type=MESH,
        ).start()
    send_unit(2)
    wait_bytes(sk.at[0, pl.ds(0, NZ - 1)], kr_sem.at[2])
    for d in (1, 3, 2):
        pltpu.make_async_remote_copy(
            src_ref=sk.at[mx],
            dst_ref=sk.at[mx],
            send_sem=ks_sem.at[3],
            recv_sem=kr_sem.at[3],
            device_id=(x_peer(d) * NZ + mz, h),
            device_id_type=MESH,
        ).start()
    send_unit(3)

    def temporal(u):
        wait_bytes(xr.at[u, pl.ds(0, NF - 1)], fr_sem.at[u])
        rows = NF * POS
        query = xr[u, :, 0].reshape(rows, HD)
        keys = xr[u, :, 1].reshape(rows, HD)
        values = xr[u, :, 2].reshape(rows, HD)
        scores = dot_nt(query, keys)
        place = lax.broadcasted_iota(jnp.int32, (rows, rows), 0) % POS
        other = lax.broadcasted_iota(jnp.int32, (rows, rows), 1) % POS
        scores = jnp.where(place == other, scores, -1e30)
        os[u] = softmax_times(scores, values).reshape(NF, POS, HD)
        if u < 2:
            g[SLOT_A, h, u, f] = os[u, f]
        else:
            tc[u - 2, f] = os[u, f]
        return_unit(u)

    def gather_y(slot, half):
        n = slot * 2 + half
        for i, d in enumerate((1, 3, 2)):
            p = lax.rem(my + d, NY) * NC + mc
            pltpu.make_async_remote_copy(
                src_ref=g.at[slot, h, half],
                dst_ref=g.at[slot, h, half],
                send_sem=ys_sem.at[n],
                recv_sem=yr_sem.at[n * 3 + i],
                device_id=(f, p),
                device_id_type=MESH,
            ).start()
        core_send(slot, half, h)

    def core_send(slot, half, p):
        n = slot * 2 + half
        pltpu.make_async_remote_copy(
            src_ref=g.at[slot, p, half],
            dst_ref=g.at[slot, p, half],
            send_sem=cs_sem.at[n],
            recv_sem=cr_sem.at[n],
            device_id=(f, my * NC + 1 - mc),
            device_id_type=MESH,
        ).start()

    def gather_core(slot, half):
        n = slot * 2 + half
        for i, d in enumerate((1, 3, 2)):
            p = lax.rem(my + NY - d, NY) * NC + mc
            wait_bytes(g.at[slot, p, half], yr_sem.at[n * 3 + i])
            core_send(slot, half, p)

    def project(slot, half, first, last):
        n = slot * 2 + half
        wait_bytes(g.at[slot, pl.ds(0, NY), half], cr_sem.at[n])
        left = jnp.concatenate([g[slot, p, half].reshape(HALF, HD) for p in range(NH)], axis=1)
        right = wg[slot].reshape(NH * HD, WID)
        part = jnp.dot(left, right, preferred_element_type=jnp.float32)
        rows = pl.ds(half * HALF, HALF)
        if not first:
            part = part + acc[rows]
        if last:
            out_ref[0, rows] = part.astype(jnp.bfloat16)
        else:
            acc[rows] = part

    temporal(0)
    wait_bytes(sk.at[pl.ds(0, NX - 1)], kr_sem.at[3])
    for s in range(2):
        for t in range(2):
            kv[s, t, pl.ds(TOK, TOK)] = sk[:, :, s, t].reshape(TOK, HD)

    block = 256

    def spatial(s, n):
        query = vq[head_of[spat[s]], pl.ds(pl.multiple_of(n * block, block), block)]
        return softmax_times(dot_nt(query, kv[s, 0]), kv[s, 1])

    per = block // POS

    def spatial_b(n, carry):
        half = n // (HALF // block)
        at = n % (HALF // block)
        g[SLOT_B, h, half, pl.ds(at * per, per)] = spatial(0, n).reshape(per, POS, HD)
        return carry

    def spatial_c(n, carry):
        half = n // (HALF // block)
        at = n % (HALF // block)
        sc[half, pl.ds(at * per, per)] = spatial(1, n).reshape(per, POS, HD)
        return carry

    lax.fori_loop(0, TOK // block, spatial_b, 0)
    gather_y(SLOT_B, 0)
    gather_y(SLOT_B, 1)
    lax.fori_loop(0, TOK // block, spatial_c, 0)

    def back_a(half):
        wait_bytes(g.at[SLOT_A, h, half, pl.ds(0, NF - 1)], br_sem.at[half])
        gather_y(SLOT_A, half)

    def back_c(half):
        wait_bytes(tc.at[half, pl.ds(0, NF - 1)], br_sem.at[2 + half])
        g[SLOT_C, h, half] = jnp.where(c_temp, tc[half], sc[half])
        gather_y(SLOT_C, half)

    temporal(1)
    back_a(0)
    gather_core(SLOT_B, 0)
    gather_core(SLOT_B, 1)
    temporal(2)
    back_a(1)
    temporal(3)
    gather_core(SLOT_A, 0)
    wait_bytes(wg.at[:, pl.ds(0, NH - 1)], wr_sem)
    back_c(0)
    project(SLOT_B, 0, True, False)
    project(SLOT_B, 1, True, False)
    gather_core(SLOT_A, 1)
    back_c(1)
    project(SLOT_A, 0, False, False)
    project(SLOT_A, 1, False, False)
    gather_core(SLOT_C, 0)
    gather_core(SLOT_C, 1)
    project(SLOT_C, 0, False, True)
    project(SLOT_C, 1, False, True)

    for u in range(4):
        wait_bytes(xs.at[u, pl.ds(0, NF - 1)], fs_sem.at[u])
        wait_bytes(os.at[u, pl.ds(0, NF - 1)], bs_sem.at[u])
    wait_bytes(ws.at[pl.ds(0, NH - 1)], ws_sem)
    wait_bytes(ss.at[pl.ds(0, NX - 1)], ks_sem.at[0])
    wait_bytes(qz.at[pl.ds(0, NZ - 1)], ks_sem.at[1])
    wait_bytes(sk.at[0, pl.ds(0, NZ - 1)], ks_sem.at[2])
    wait_bytes(sk.at[pl.ds(0, NX - 1)], ks_sem.at[3])
    for n in range(6):
        wait_bytes(g.at[0, pl.ds(0, NY - 1), 0], ys_sem.at[n])
        wait_bytes(g.at[0, pl.ds(0, NY), 0], cs_sem.at[n])


def per_device(queries, keys, values, out_weight, head_class, sink_frame):
    bf16, f32 = jnp.bfloat16, jnp.float32
    dma = pltpu.SemaphoreType.DMA
    spread = pltpu.VMEM
    return pl.pallas_call(
        kernel,
        out_shape=jax.ShapeDtypeStruct((1, TOK, WID), bf16),
        in_specs=[pl.BlockSpec(memory_space=pltpu.SMEM)] * 2
        + [pl.BlockSpec(memory_space=pl.ANY)] * 4,
        out_specs=pl.BlockSpec(memory_space=pltpu.VMEM),
        scratch_shapes=[
            spread((3, TOK, HD), bf16),
            spread((3, TOK, HD), bf16),
            spread((3, TOK, HD), bf16),
            spread((3, HD, NH * WID), bf16),
            spread((4, NF, 3, POS, HD), bf16),
            spread((4, NF, 3, POS, HD), bf16),
            spread((4, NF, POS, HD), bf16),
            spread((2, NF, POS, HD), bf16),
            spread((3, NH, 2, NF, POS, HD), bf16),
            spread((NH, 3, HD, WID), bf16),
            spread((3, NH, HD, WID), bf16),
            spread((TOK, WID), f32),
            spread((NX, 2, 2, TOK // NX, HD), bf16),
            spread((NX, 2, 2, TOK // NX, HD), bf16),
            spread((NZ, 2, 2, TOK // NF, HD), bf16),
            spread((NZ, 2, 2, TOK // NF, HD), bf16),
            spread((NX, NZ, 2, 2, TOK // NF, HD), bf16),
            spread((2, 2, 2 * TOK, HD), bf16),
            spread((2, NF, POS, HD), bf16),
            dma((12,)),
            dma((4,)),
            dma((4,)),
            dma((4,)),
            dma((4,)),
            dma,
            dma,
            dma((4,)),
            dma((4,)),
            dma((6,)),
            dma((18,)),
            dma((6,)),
            dma((6,)),
        ],
        compiler_params=pltpu.CompilerParams(
            collective_id=0, has_side_effects=True, vmem_limit_bytes=56 * 2**20
        ),
        cost_estimate=pl.CostEstimate(
            flops=7 * 10**9, bytes_accessed=8 * 10**6, transcendentals=6 * 10**6
        ),
    )(head_class, sink_frame, queries, keys, values, out_weight)


def solution(mesh):
    placed = (
        P("frame", None, "head"),
        P("frame", None, "head"),
        P("frame", None, "head"),
        P("head", None),
        P("head"),
        P("head"),
    )
    return jax.shard_map(
        per_device, mesh=mesh, in_specs=placed, out_specs=P("frame", None, "head"), check_vma=False
    )
```

time: 381 us -> 113 us (0.30)
  waiting for transfers between devices: 230 us -> 0 us
  Pallas kernels: 0 us -> 110 us
  starting transfers between devices: 38.2 us -> 0 us
  local copies, waits for them, and re-layouts: 36.7 us -> 2.09 us
  matrix products: 32.5 us -> 0 us
  between operations: 23.1 us -> 0.01 us
  other arithmetic: 18.6 us -> 0 us
    psum x1 -> x0, waiting for transfers between devices: 134 us -> none  [broadcast(): return lax.psum(kept, axis)]
    pallas_call x0 -> x1, Pallas kernels: none -> 110 us  [per_device(): pl.pallas_call(kernel, out_shape=jax.ShapeDtypeStruct((1, TOK, WID), bf16...]
    all_to_all x4 -> x0, waiting for transfers between devices: 50.6 us -> none  [the longest x1 22 us: per_device(): lax.all_to_all(pick_heads(local_k, order, head_dim)[None], 'frame', split...]
    unnamed x3 -> x0, waiting for transfers between devices: 46.2 us -> none
    all_to_all x4 -> x0, starting transfers between devices: 37.9 us -> none  [the longest x1 12 us: per_device(): lax.all_to_all(pick_heads(local_q, order, head_dim)[None], 'frame', split...]
    dot_general x17 -> x0, matrix products: 32.5 us -> none  [the longest x6 6.68 us: attend(): scores = jnp.dot(query, keys.T, preferred_element_type=jnp.float32) * scale]
    unnamed x12 -> x1, local copies, waits for them, and re-layouts: 12.8 us -> 2.09 us
    concatenate x6 -> x0, other arithmetic: 8.76 us -> none  [the longest x3 5.57 us: per_device(): values_one = jnp.concatenate([spat_v[:, slot], sink_v], axis=0)]
  transfers between devices with their start and end apart: 6 -> 0, of which waited for: 5 -> 0; matrix products, arithmetic and copies ran while one was open for 15% -> 0% of each run, Pallas kernels for 0% -> 0%
where the time goes in v1:
time: 113 us
  Pallas kernels  110 us (97%)
  local copies, waits for them, and re-layouts  2.09 us (2%)
    pallas_call x1, Pallas kernels, per_device(): pl.pallas_call(kernel, out_shape=jax.ShapeDtypeStruct((1, TOK, WID), bf16...  110 us

profile of v1, /device:TPU:1, one launch (start us, length us, event | category | flops | bytes accessed | tf_op | source)
XLA Modules:
  0.0 112.6 jit_solution(12144388199999012140)
XLA Ops:
  0.0 110.5 %shard_map.64 = bf16[1,1024,384]{2,1,0:T(8,128)(2,1)} custom-call(s32[3]{0:T(128)} %cls.1, s32[3]{0:T(128)} %sink.1, bf16[1,1024,384]{2,1,0:T(8,128)(2,1)} %q_hbm.1, bf16[1,1024,384]{2,1,0:T(8,128)(2,1)} %k_hbm.1, bf16[1,1024,384]{2,1,0:T(8,128)(2,1)} %v_hbm.1, bf16[384,3072]{1,0:T(8,128)(2,1)} %w_hbm.1), custom_call_target="tpu_custom_call" | custom-call | flops 7000000000 | bytes 8000000 | tf_op jit(solution)/shard_map/pallas_call | solution.py:393
  110.5 2.1 %copy.8 = bf16[1,1024,384]{2,1,0:T(8,128)(2,1)} copy(bf16[1,1024,384]{2,1,0:T(8,128)(2,1)} %shard_map.64) | data formatting | bytes 1572864

commit v2 on v1

v2 whole, which is shorter than its diff:
```python
import math

import jax
import jax.numpy as jnp
from jax import lax
from jax.experimental import pallas as pl
from jax.experimental.pallas import tpu as pltpu
from jax.sharding import PartitionSpec as P

MESH = pl.DeviceIdType.MESH
NX, NZ, NY, NC = 4, 8, 4, 2
NF, NH = NX * NZ, NY * NC
TOK, HD, WID = 1024, 128, 384
HALF = TOK // 2
POS = HALF // NF
SLOT_A, SLOT_C, SLOT_B = 0, 1, 2
SCALE = HD ** (-0.5) * math.log2(math.e)


def first_with(cls, kind):
    return jnp.where(cls[0] == kind, 0, jnp.where(cls[1] == kind, 1, 2))


def softmax_times(scores, values):
    top = jnp.max(scores, axis=-1, keepdims=True)
    weights = jnp.exp2((scores - top) * SCALE)
    total = jnp.sum(weights, axis=-1, keepdims=True)
    mixed = jnp.dot(weights.astype(jnp.bfloat16), values, preferred_element_type=jnp.float32)
    return (mixed / total).astype(jnp.bfloat16)


def dot_nt(a, b):
    return lax.dot_general(a, b, (((1,), (1,)), ((), ())), preferred_element_type=jnp.float32)


def kernel(
    cls,
    sink,
    q_hbm,
    k_hbm,
    v_hbm,
    w_hbm,
    out_ref,
    vq,
    vk,
    vv,
    vw,
    xa,
    ra,
    xk,
    rk,
    xq,
    rq,
    os,
    tc,
    g,
    ws,
    wg,
    acc,
    ss,
    rx,
    qz,
    rz,
    sk,
    kv,
    sc,
    in_sem,
    fs_sem,
    fr_sem,
    bs_sem,
    br_sem,
    ws_sem,
    wr_sem,
    ks_sem,
    kr_sem,
    ys_sem,
    yr_sem,
    cs_sem,
    cr_sem,
):
    f = lax.axis_index("frame")
    h = lax.axis_index("head")
    mx, mz, my, mc = f // NZ, f % NZ, h // NC, h % NC

    ins = []
    for n, (src, dst) in enumerate(((k_hbm, vk), (v_hbm, vv), (q_hbm, vq))):
        for j in range(3):
            cp = pltpu.make_async_copy(
                src.at[0, :, pl.ds(j * HD, HD)], dst.at[j], in_sem.at[n * 3 + j]
            )
            cp.start()
            ins.append(cp)
    for j in range(3):
        cp = pltpu.make_async_copy(w_hbm.at[pl.ds(j * HD, HD)], vw.at[j], in_sem.at[9 + j])
        cp.start()
        ins.append(cp)

    barrier = pltpu.get_barrier_semaphore()

    def greet_frame(d, carry):
        pl.semaphore_signal(
            barrier, inc=1, device_id=(lax.rem(f + d, NF), h), device_id_type=MESH
        )
        return carry

    def greet_head(d, carry):
        pl.semaphore_signal(
            barrier, inc=1, device_id=(f, lax.rem(h + d, NH)), device_id_type=MESH
        )
        return carry

    lax.fori_loop(1, NF, greet_frame, 0)
    lax.fori_loop(1, NH, greet_head, 0)

    ia = first_with(cls, 1)
    ib = first_with(cls, 0)
    ic = 3 - ia - ib
    c_temp = cls[ic] == 1
    head_of = {SLOT_A: ia, SLOT_B: ib, SLOT_C: ic}
    spat = (SLOT_B, SLOT_C)
    root_b, root_c = sink[ib], sink[ic]

    def wait_bytes(ref, sem):
        pltpu.make_async_copy(ref, ref, sem).wait()

    def x_peer(d):
        return lax.rem(mx + d, NX)

    def z_peer(d):
        return lax.rem(mz + d, NZ)

    def to_frames(src, dst, send_sem, recv_sem):
        def one(d, carry):
            p = lax.rem(f + d, NF)
            pltpu.make_async_remote_copy(
                src_ref=src.at[p],
                dst_ref=dst,
                send_sem=send_sem,
                recv_sem=recv_sem,
                device_id=(p, h),
                device_id_type=MESH,
            ).start()
            return carry

        lax.fori_loop(1, NF, one, 0)

    def to_x(src, dst, n):
        for d in (1, 3, 2):
            pltpu.make_async_remote_copy(
                src_ref=src(x_peer(d)),
                dst_ref=dst,
                send_sem=ks_sem.at[n],
                recv_sem=kr_sem.at[n],
                device_id=(x_peer(d) * NZ + mz, h),
                device_id_type=MESH,
            ).start()

    def to_z(src, dst, n):
        for d in (1, 7, 2, 6, 3, 5, 4):
            pltpu.make_async_remote_copy(
                src_ref=src(z_peer(d)),
                dst_ref=dst,
                send_sem=ks_sem.at[n],
                recv_sem=kr_sem.at[n],
                device_id=(mx * NZ + z_peer(d), h),
                device_id_type=MESH,
            ).start()

    for n in range(6):
        ins[n].wait()
    ss[:, 0] = vk[ib].reshape(NX, TOK // NX, HD)
    ss[:, 1] = vv[ib].reshape(NX, TOK // NX, HD)
    for t, src in enumerate((vk, vv)):
        for half in range(2):
            xk[:, t, half] = src[ic, pl.ds(half * HALF, HALF)].reshape(NF, POS, HD)
    pl.semaphore_wait(barrier, NF - 1 + NH - 1)
    to_x(lambda p: ss.at[p], rx.at[mx], 0)
    rx[mx] = ss[mx]
    rk[f] = xk[f]

    for n in range(9, 12):
        ins[n].wait()
    for slot in (SLOT_A, SLOT_C, SLOT_B):
        for p in range(NH):
            ws[p, slot] = vw[head_of[slot], :, pl.ds(p * WID, WID)]
        wg[slot, h] = ws[h, slot]

    def send_weights(d, carry):
        p = lax.rem(h + d, NH)
        pltpu.make_async_remote_copy(
            src_ref=ws.at[p],
            dst_ref=wg.at[:, h],
            send_sem=ws_sem,
            recv_sem=wr_sem,
            device_id=(f, p),
            device_id_type=MESH,
        ).start()
        return carry

    lax.fori_loop(1, NH, send_weights, 0)
    to_frames(xk, rk.at[f], fs_sem.at[2], fr_sem.at[2])

    for n in range(6, 9):
        ins[n].wait()
    for half in range(2):
        for t, src in enumerate((vq, vk, vv)):
            xa[half, :, t] = src[ia, pl.ds(half * HALF, HALF)].reshape(NF, POS, HD)
        ra[half, f] = xa[half, f]
        xq[half] = vq[ic, pl.ds(half * HALF, HALF)].reshape(NF, POS, HD)
        rq[half, f] = xq[half, f]
    for s, slot in enumerate(spat):
        kv[s, 0, pl.ds(0, TOK)] = vk[head_of[slot]]
        kv[s, 1, pl.ds(0, TOK)] = vv[head_of[slot]]

    def send_a(half):
        to_frames(xa.at[half], ra.at[half, f], fs_sem.at[half], fr_sem.at[half])

    def send_q(half):
        to_frames(xq.at[half], rq.at[half, f], fs_sem.at[3 + half], fr_sem.at[3 + half])

    wait_bytes(rx.at[pl.ds(0, NX - 1)], kr_sem.at[0])
    for t in range(2):
        qz[:, t] = rx[root_b // NZ, t].reshape(NZ, TOK // NF, HD)
    rz[mz] = qz[mz]
    to_z(lambda p: qz.at[p], rz.at[mz], 1)
    wait_bytes(rz.at[pl.ds(0, NZ - 1)], kr_sem.at[1])
    sk[0, mx, mz] = rz[root_b % NZ]
    to_z(lambda p: sk.at[0, mx, mz], sk.at[0, mx, mz], 2)
    wait_bytes(rk.at[pl.ds(0, NF - 1)], fr_sem.at[2])
    sk[1, mx, mz] = rk[root_c].reshape(2, 2 * POS, HD)
    to_z(lambda p: sk.at[1, mx, mz], sk.at[1, mx, mz], 3)
    send_a(0)
    wait_bytes(sk.at[0, 0, pl.ds(0, NZ - 1)], kr_sem.at[2])
    to_x(lambda p: sk.at[0, mx], sk.at[0, mx], 4)
    wait_bytes(sk.at[1, 0, pl.ds(0, NZ - 1)], kr_sem.at[3])
    to_x(lambda p: sk.at[1, mx], sk.at[1, mx], 5)
    send_a(1)

    def attend_positions(query, keys, values, u):
        rows = NF * POS
        query, keys, values = (a.reshape(rows, HD) for a in (query, keys, values))
        scores = dot_nt(query, keys)
        place = lax.broadcasted_iota(jnp.int32, (rows, rows), 0) % POS
        other = lax.broadcasted_iota(jnp.int32, (rows, rows), 1) % POS
        scores = jnp.where(place == other, scores, -1e30)
        os[u] = softmax_times(scores, values).reshape(NF, POS, HD)

    def temporal_a(half):
        wait_bytes(ra.at[half, pl.ds(0, NF - 1)], fr_sem.at[half])
        attend_positions(ra[half, :, 0], ra[half, :, 1], ra[half, :, 2], half)
        g[SLOT_A, h, half, f] = os[half, f]
        to_frames(os.at[half], g.at[SLOT_A, h, half, f], bs_sem.at[half], br_sem.at[half])

    def temporal_c(half):
        wait_bytes(rq.at[half, pl.ds(0, NF - 1)], fr_sem.at[3 + half])
        attend_positions(rq[half], rk[:, 0, half], rk[:, 1, half], 2 + half)
        tc[half, f] = os[2 + half, f]
        to_frames(os.at[2 + half], tc.at[half, f], bs_sem.at[2 + half], br_sem.at[2 + half])

    def core_send(slot, half, p):
        n = slot * 2 + half
        pltpu.make_async_remote_copy(
            src_ref=g.at[slot, p, half],
            dst_ref=g.at[slot, p, half],
            send_sem=cs_sem.at[n],
            recv_sem=cr_sem.at[n],
            device_id=(f, my * NC + 1 - mc),
            device_id_type=MESH,
        ).start()

    up = lax.rem(my + 1, NY) * NC + mc
    down = lax.rem(my + NY - 1, NY) * NC + mc
    across = lax.rem(my + 2, NY) * NC + mc

    def y_send(ref, n, i, p):
        pltpu.make_async_remote_copy(
            src_ref=ref,
            dst_ref=ref,
            send_sem=ys_sem.at[n],
            recv_sem=yr_sem.at[n * 3 + i],
            device_id=(f, p),
            device_id_type=MESH,
        ).start()

    def gather_y(slot, half):
        n = slot * 2 + half
        y_send(g.at[slot, h, half], n, 0, up)
        y_send(g.at[slot, h, half], n, 1, down)
        core_send(slot, half, h)

    def pass_on(slot, half):
        n = slot * 2 + half
        wait_bytes(g.at[slot, down, half], yr_sem.at[n * 3])
        y_send(g.at[slot, down, half, pl.ds(0, NF // 2)], n, 2, up)
        core_send(slot, half, down)
        wait_bytes(g.at[slot, up, half], yr_sem.at[n * 3 + 1])
        y_send(g.at[slot, up, half, pl.ds(NF // 2, NF // 2)], n, 2, down)
        core_send(slot, half, up)

    def gather_core(slot, half):
        n = slot * 2 + half
        wait_bytes(g.at[slot, across, half], yr_sem.at[n * 3 + 2])
        core_send(slot, half, across)

    def project(slot, half, first, last):
        n = slot * 2 + half
        wait_bytes(g.at[slot, pl.ds(0, NY), half], cr_sem.at[n])
        left = jnp.concatenate([g[slot, p, half].reshape(HALF, HD) for p in range(NH)], axis=1)
        right = wg[slot].reshape(NH * HD, WID)
        part = jnp.dot(left, right, preferred_element_type=jnp.float32)
        rows = pl.ds(half * HALF, HALF)
        if not first:
            part = part + acc[rows]
        if last:
            out_ref[0, rows] = part.astype(jnp.bfloat16)
        else:
            acc[rows] = part

    block = 256
    per = block // POS

    def spatial(s, n):
        query = vq[head_of[spat[s]], pl.ds(pl.multiple_of(n * block, block), block)]
        return softmax_times(dot_nt(query, kv[s, 0]), kv[s, 1]).reshape(per, POS, HD)

    def spatial_b(half):
        def one(n, carry):
            g[SLOT_B, h, half, pl.ds(n * per, per)] = spatial(0, half * (HALF // block) + n)
            return carry

        lax.fori_loop(0, HALF // block, one, 0)

    def spatial_c(half):
        def one(n, carry):
            sc[half, pl.ds(n * per, per)] = spatial(1, half * (HALF // block) + n)
            return carry

        lax.fori_loop(0, HALF // block, one, 0)

    def back_a(half):
        wait_bytes(g.at[SLOT_A, h, half, pl.ds(0, NF - 1)], br_sem.at[half])
        gather_y(SLOT_A, half)

    def back_c(half):
        wait_bytes(tc.at[half, pl.ds(0, NF - 1)], br_sem.at[2 + half])
        g[SLOT_C, h, half] = jnp.where(c_temp, tc[half], sc[half])
        gather_y(SLOT_C, half)

    def sink_ready(s):
        wait_bytes(sk.at[s, pl.ds(0, NX - 1)], kr_sem.at[4 + s])
        for t in range(2):
            kv[s, t, pl.ds(TOK, TOK)] = sk[s, :, :, t].reshape(TOK, HD)

    temporal_a(0)
    send_q(0)
    send_q(1)
    sink_ready(0)
    spatial_b(0)
    gather_y(SLOT_B, 0)
    spatial_b(1)
    gather_y(SLOT_B, 1)
    temporal_a(1)
    back_a(0)
    sink_ready(1)
    spatial_c(0)
    pass_on(SLOT_B, 0)
    spatial_c(1)
    pass_on(SLOT_B, 1)
    temporal_c(0)
    gather_core(SLOT_B, 0)
    temporal_c(1)
    pass_on(SLOT_A, 0)
    gather_core(SLOT_B, 1)
    back_a(1)
    gather_core(SLOT_A, 0)
    back_c(0)
    pass_on(SLOT_A, 1)
    wait_bytes(wg.at[:, pl.ds(0, NH - 1)], wr_sem)
    project(SLOT_B, 0, True, False)
    back_c(1)
    pass_on(SLOT_C, 0)
    gather_core(SLOT_A, 1)
    project(SLOT_A, 0, False, False)
    pass_on(SLOT_C, 1)
    gather_core(SLOT_C, 0)
    project(SLOT_B, 1, True, False)
    gather_core(SLOT_C, 1)
    project(SLOT_A, 1, False, False)
    project(SLOT_C, 0, False, True)
    project(SLOT_C, 1, False, True)

    for half in range(2):
        wait_bytes(xa.at[half, pl.ds(0, NF - 1)], fs_sem.at[half])
        wait_bytes(xq.at[half, pl.ds(0, NF - 1)], fs_sem.at[3 + half])
    wait_bytes(xk.at[pl.ds(0, NF - 1)], fs_sem.at[2])
    for u in range(4):
        wait_bytes(os.at[u, pl.ds(0, NF - 1)], bs_sem.at[u])
    wait_bytes(ws.at[pl.ds(0, NH - 1)], ws_sem)
    wait_bytes(ss.at[pl.ds(0, NX - 1)], ks_sem.at[0])
    wait_bytes(qz.at[pl.ds(0, NZ - 1)], ks_sem.at[1])
    for s in range(2):
        wait_bytes(sk.at[s, 0, pl.ds(0, NZ - 1)], ks_sem.at[2 + s])
        wait_bytes(sk.at[s, pl.ds(0, NX - 1)], ks_sem.at[4 + s])
    for n in range(6):
        wait_bytes(g.at[0, pl.ds(0, NY - 1), 0], ys_sem.at[n])
        wait_bytes(g.at[0, pl.ds(0, NY), 0], cs_sem.at[n])


def per_device(queries, keys, values, out_weight, head_class, sink_frame):
    bf16, f32 = jnp.bfloat16, jnp.float32
    dma = pltpu.SemaphoreType.DMA
    spread = pltpu.VMEM
    return pl.pallas_call(
        kernel,
        out_shape=jax.ShapeDtypeStruct((1, TOK, WID), bf16),
        in_specs=[pl.BlockSpec(memory_space=pltpu.SMEM)] * 2
        + [pl.BlockSpec(memory_space=pl.ANY)] * 4,
        out_specs=pl.BlockSpec(memory_space=pltpu.VMEM),
        scratch_shapes=[
            spread((3, TOK, HD), bf16),
            spread((3, TOK, HD), bf16),
            spread((3, TOK, HD), bf16),
            spread((3, HD, NH * WID), bf16),
            spread((2, NF, 3, POS, HD), bf16),
            spread((2, NF, 3, POS, HD), bf16),
            spread((NF, 2, 2, POS, HD), bf16),
            spread((NF, 2, 2, POS, HD), bf16),
            spread((2, NF, POS, HD), bf16),
            spread((2, NF, POS, HD), bf16),
            spread((4, NF, POS, HD), bf16),
            spread((2, NF, POS, HD), bf16),
            spread((3, NH, 2, NF, POS, HD), bf16),
            spread((NH, 3, HD, WID), bf16),
            spread((3, NH, HD, WID), bf16),
            spread((TOK, WID), f32),
            spread((NX, 2, TOK // NX, HD), bf16),
            spread((NX, 2, TOK // NX, HD), bf16),
            spread((NZ, 2, TOK // NF, HD), bf16),
            spread((NZ, 2, TOK // NF, HD), bf16),
            spread((2, NX, NZ, 2, TOK // NF, HD), bf16),
            spread((2, 2, 2 * TOK, HD), bf16),
            spread((2, NF, POS, HD), bf16),
            dma((12,)),
            dma((5,)),
            dma((5,)),
            dma((4,)),
            dma((4,)),
            dma,
            dma,
            dma((6,)),
            dma((6,)),
            dma((6,)),
            dma((18,)),
            dma((6,)),
            dma((6,)),
        ],
        compiler_params=pltpu.CompilerParams(
            collective_id=0, has_side_effects=True, vmem_limit_bytes=56 * 2**20
        ),
        cost_estimate=pl.CostEstimate(
            flops=7 * 10**9, bytes_accessed=8 * 10**6, transcendentals=6 * 10**6
        ),
    )(head_class, sink_frame, queries, keys, values, out_weight)


def solution(mesh):
    placed = (
        P("frame", None, "head"),
        P("frame", None, "head"),
        P("frame", None, "head"),
        P("head", None),
        P("head"),
        P("head"),
    )
    return jax.shard_map(
        per_device, mesh=mesh, in_specs=placed, out_specs=P("frame", None, "head"), check_vma=False
    )
```

time: 113 us -> 90.4 us (0.80)
  Pallas kernels: 110 us -> 88.2 us
    pallas_call x1, Pallas kernels: 110 us -> 88.2 us  [per_device(): pl.pallas_call(kernel, out_shape=jax.ShapeDtypeStruct((1, TOK, WID), bf16...]
where the time goes in v2:
time: 90.4 us; the launch traced here: 90.3 us
  Pallas kernels  88.2 us (98%)
  local copies, waits for them, and re-layouts  2.09 us (2%)
    pallas_call x1, Pallas kernels, per_device(): pl.pallas_call(kernel, out_shape=jax.ShapeDtypeStruct((1, TOK, WID), bf16...  88.2 us
    unnamed x1, local copies, waits for them, and re-layouts  2.09 us

profile of v2, /device:TPU:1, one launch (start us, length us, event | category | flops | bytes accessed | tf_op | source)
XLA Modules:
  0.0 90.3 jit_solution(282056745473424953)
XLA Ops:
  0.0 88.2 %shard_map.64 = bf16[1,1024,384]{2,1,0:T(8,128)(2,1)} custom-call(s32[3]{0:T(128)} %cls.1, s32[3]{0:T(128)} %sink.1, bf16[1,1024,384]{2,1,0:T(8,128)(2,1)} %q_hbm.1, bf16[1,1024,384]{2,1,0:T(8,128)(2,1)} %k_hbm.1, bf16[1,1024,384]{2,1,0:T(8,128)(2,1)} %v_hbm.1, bf16[384,3072]{1,0:T(8,128)(2,1)} %w_hbm.1), custom_call_target="tpu_custom_call" | custom-call | flops 7000000000 | bytes 8000000 | tf_op jit(solution)/shard_map/pallas_call | solution.py:413
  88.2 2.1 %copy.8 = bf16[1,1024,384]{2,1,0:T(8,128)(2,1)} copy(bf16[1,1024,384]{2,1,0:T(8,128)(2,1)} %shard_map.64) | data formatting | bytes 1572864

commit v3 on v2

--- a/solution.py
+++ b/solution.py
@@ -131,7 +131,7 @@
 
     def to_frames(src, dst, send_sem, recv_sem):
         def one(d, carry):
-            p = lax.rem(f + d, NF)
+            p = lax.rem(f + lax.rem(d, 2) * ((d + 1) // 2) + (1 - lax.rem(d, 2)) * (NF - d // 2), NF)
             pltpu.make_async_remote_copy(
                 src_ref=src.at[p],
                 dst_ref=dst,
@@ -368,10 +368,10 @@
     pass_on(SLOT_B, 1)
     temporal_c(0)
     gather_core(SLOT_B, 0)
-    temporal_c(1)
     pass_on(SLOT_A, 0)
     gather_core(SLOT_B, 1)
     back_a(1)
+    temporal_c(1)
     gather_core(SLOT_A, 0)
     back_c(0)
     pass_on(SLOT_A, 1)

time: 90.4 us -> 89.3 us (0.988)
  Pallas kernels: 88.2 us -> 87.1 us
    pallas_call x1, Pallas kernels: 88.2 us -> 87.1 us  [per_device(): pl.pallas_call(kernel, out_shape=jax.ShapeDtypeStruct((1, TOK, WID), bf16...]
where the time goes in v3:
time: 89.3 us; the launch traced here: 89.2 us
  Pallas kernels  87.1 us (98%)
  local copies, waits for them, and re-layouts  2.09 us (2%)
    pallas_call x1, Pallas kernels, per_device(): pl.pallas_call(kernel, out_shape=jax.ShapeDtypeStruct((1, TOK, WID), bf16...  87.1 us
    unnamed x1, local copies, waits for them, and re-layouts  2.09 us

profile of v3, /device:TPU:1, one launch (start us, length us, event | category | flops | bytes accessed | tf_op | source)
XLA Modules:
  0.0 89.2 jit_solution(7364883891309543690)
XLA Ops:
  0.0 87.1 %shard_map.64 = bf16[1,1024,384]{2,1,0:T(8,128)(2,1)} custom-call(s32[3]{0:T(128)} %cls.1, s32[3]{0:T(128)} %sink.1, bf16[1,1024,384]{2,1,0:T(8,128)(2,1)} %q_hbm.1, bf16[1,1024,384]{2,1,0:T(8,128)(2,1)} %k_hbm.1, bf16[1,1024,384]{2,1,0:T(8,128)(2,1)} %v_hbm.1, bf16[384,3072]{1,0:T(8,128)(2,1)} %w_hbm.1), custom_call_target="tpu_custom_call" | custom-call | flops 7000000000 | bytes 8000000 | tf_op jit(solution)/shard_map/pallas_call | solution.py:413
  87.1 2.1 %copy.8 = bf16[1,1024,384]{2,1,0:T(8,128)(2,1)} copy(bf16[1,1024,384]{2,1,0:T(8,128)(2,1)} %shard_map.64) | data formatting | bytes 1572864

commit v4 on v3

--- a/solution.py
+++ b/solution.py
@@ -131,7 +131,8 @@
 
     def to_frames(src, dst, send_sem, recv_sem):
         def one(d, carry):
-            p = lax.rem(f + lax.rem(d, 2) * ((d + 1) // 2) + (1 - lax.rem(d, 2)) * (NF - d // 2), NF)
+            e = NF - d
+            p = lax.rem(f + lax.rem(e, 2) * ((e + 1) // 2) + (1 - lax.rem(e, 2)) * (NF - e // 2), NF)
             pltpu.make_async_remote_copy(
                 src_ref=src.at[p],
                 dst_ref=dst,

time: 89.3 us -> 90.4 us (1.012)
  Pallas kernels: 87.1 us -> 88.2 us
    pallas_call x1, Pallas kernels: 87.1 us -> 88.2 us  [per_device(): pl.pallas_call(kernel, out_shape=jax.ShapeDtypeStruct((1, TOK, WID), bf16...]
where the time goes in v4:
time: 90.4 us; the launch traced here: 90.3 us
  Pallas kernels  88.2 us (98%)
  local copies, waits for them, and re-layouts  2.09 us (2%)
    pallas_call x1, Pallas kernels, per_device(): pl.pallas_call(kernel, out_shape=jax.ShapeDtypeStruct((1, TOK, WID), bf16...  88.2 us
    unnamed x1, local copies, waits for them, and re-layouts  2.09 us

profile of v4, /device:TPU:1, one launch (start us, length us, event | category | flops | bytes accessed | tf_op | source)
XLA Modules:
  0.0 90.3 jit_solution(9262511371137937088)
XLA Ops:
  0.0 88.2 %shard_map.64 = bf16[1,1024,384]{2,1,0:T(8,128)(2,1)} custom-call(s32[3]{0:T(128)} %cls.1, s32[3]{0:T(128)} %sink.1, bf16[1,1024,384]{2,1,0:T(8,128)(2,1)} %q_hbm.1, bf16[1,1024,384]{2,1,0:T(8,128)(2,1)} %k_hbm.1, bf16[1,1024,384]{2,1,0:T(8,128)(2,1)} %v_hbm.1, bf16[384,3072]{1,0:T(8,128)(2,1)} %w_hbm.1), custom_call_target="tpu_custom_call" | custom-call | flops 7000000000 | bytes 8000000 | tf_op jit(solution)/shard_map/pallas_call | solution.py:414
  88.2 2.1 %copy.8 = bf16[1,1024,384]{2,1,0:T(8,128)(2,1)} copy(bf16[1,1024,384]{2,1,0:T(8,128)(2,1)} %shard_map.64) | data formatting | bytes 1572864
